TPU v7x, 32 devices: a whole 2x2x4 slice. The times are simulated.
32 devices in a mesh: clip: 4 (over y, x), frame: 8 (over z, core).
Axes of the slice: x: 2, y: 2, z: 4, core: 2. Of those that a mesh axis runs over, the one named last changes fastest.
Arguments:
- hidden_in: bfloat16 [8, 1024, 1024], P('clip', 'frame'), may hold values from -6 to 6
- text_states: bfloat16 [8, 128, 1024], P('clip'), may hold values from -6 to 6
- out_grad: bfloat16 [8, 1024, 1024], P('clip', 'frame'), may hold values from -6 to 6
- self_qkv: bfloat16 [1024, 3, 1024], P(('clip', 'frame')), may hold values from -0.1875 to 0.1875
- self_out: bfloat16 [1024, 1024], P(('clip', 'frame')), may hold values from -1 to 1
- cross_qkv: bfloat16 [1024, 3, 1024], P(('clip', 'frame')), may hold values from -0.1875 to 0.1875
- cross_out: bfloat16 [1024, 1024], P(('clip', 'frame')), may hold values from -0.5 to 0.5
- ffn_in: bfloat16 [1024, 4096], P(('clip', 'frame')), may hold values from -0.1875 to 0.1875
- ffn_out: bfloat16 [4096, 1024], P(('clip', 'frame')), may hold values from -0.09375 to 0.09375
- ln_gain: bfloat16 [3, 1024], P(None, ('clip', 'frame')), may hold values from 0.5 to 1.5
- ln_bias: bfloat16 [3, 1024], P(None, ('clip', 'frame')), may hold values from -3 to 3
- clip_len: int32 [8], P('clip'), may hold values from 170 to 1024, as said below
- frame_mask: int32 [8, 1024], P('clip'), may hold values 0 or 1
- text_len: int32 [8], P('clip'), may hold values from 5 to 120
- text_mask: int32 [8, 128], P('clip'), may hold values 0 or 1
Outputs:
- output: bfloat16 [8, 1024, 1024], P('clip', 'frame')
- grad_hidden: bfloat16 [8, 1024, 1024], P('clip', 'frame')
- grad_text: bfloat16 [8, 128, 1024], P('clip', 'frame')
- grad_self_qkv: float32 [1024, 3, 1024], P(('clip', 'frame'))
- grad_self_out: float32 [1024, 1024], P(('clip', 'frame'))
- grad_cross_qkv: float32 [1024, 3, 1024], P(('clip', 'frame'))
- grad_cross_out: float32 [1024, 1024], P(('clip', 'frame'))
- grad_ffn_in: float32 [1024, 4096], P(('clip', 'frame'))
- grad_ffn_out: float32 [4096, 1024], P(('clip', 'frame'))
- grad_ln_gain: float32 [3, 1024], P(None, ('clip', 'frame'))
- grad_ln_bias: float32 [3, 1024], P(None, ('clip', 'frame'))
Inputs may be any that keep to these rules, and one draw needn't show every extreme that they name: `clip_len`: in every aligned group of 2 clips at least one has the full length 1024.
All inputs are finite; a program needn't handle non-finite values. No bound on the sum of `frame_mask` or of `text_mask` on one device may be relied on, other than what follows from the above.
Results may differ from a plain program's by a relative error of at most 0.019.
Values may be sent and summed in bfloat16 or wider, within the bound.
A program may use at most 320 MiB of HBM per device.

v0:
```python
import functools

import jax
import jax.numpy as jnp
from jax import lax
from jax.experimental import pallas as pl
from jax.experimental.pallas import tpu as pltpu
from jax.sharding import PartitionSpec as P

HD = 64


MASKED = -1000000000.0
EPSILON = 1e-05


def layer_norm(value, gain, shift):
    average = jnp.mean(value, axis=-1, keepdims=True)
    centered = value - average
    variance = jnp.mean(centered * centered, axis=-1, keepdims=True)
    return centered * lax.rsqrt(variance + EPSILON) * gain + shift


def activate(value):
    return jax.nn.gelu(value, approximate=False)


def project(left, right):
    return jnp.einsum("cnd,de->cne", left, right, preferred_element_type=jnp.float32)


def project_back(grad_rows, weight):
    return jnp.einsum("cne,de->cnd", grad_rows, weight, preferred_element_type=jnp.float32)


def weight_grad(left, right):
    return jnp.einsum("cnd,cne->de", left, right, preferred_element_type=jnp.float32)


def fetch_attention(self_qkv, self_out, cross_qkv, cross_out, ln_gain, ln_bias):
    return (
        lax.all_gather(self_qkv, ("clip", "frame"), axis=0, tiled=True),
        lax.all_gather(self_out, ("clip", "frame"), axis=0, tiled=True),
        lax.all_gather(cross_qkv, ("clip", "frame"), axis=0, tiled=True),
        lax.all_gather(cross_out, ("clip", "frame"), axis=0, tiled=True),
        lax.all_gather(ln_gain, ("clip", "frame"), axis=1, tiled=True),
        lax.all_gather(ln_bias, ("clip", "frame"), axis=1, tiled=True),
    )


def fetch_ffn(ffn_in, ffn_out):
    return (
        lax.all_gather(ffn_in, ("clip", "frame"), axis=0, tiled=True),
        lax.all_gather(ffn_out, ("clip", "frame"), axis=0, tiled=True),
    )


def self_masks(first_row, block_rows, clip_len, key_valid):
    columns = jnp.arange(key_valid.shape[1], dtype=jnp.int32)
    row_ids = first_row + jnp.arange(block_rows, dtype=jnp.int32)
    diagonal = columns[None, :] == row_ids[:, None]
    allowed = (columns[None, :] <= row_ids[:, None])[None] & (
        key_valid[:, None, :] | diagonal[None]
    )
    live_rows = (row_ids[None, :] < clip_len[:, None]).astype(jnp.float32)
    return (allowed[:, None], live_rows[:, None, :, None])


def self_forward(query_rows, key_rows, value_rows, clip_len, key_valid):
    length = query_rows.shape[1]
    block_rows = min(512, length)
    score_scale = query_rows.shape[3] ** (-0.5)

    def one_block(block_index):
        first_row = block_index * block_rows
        query_block = lax.dynamic_slice_in_dim(query_rows, first_row, block_rows, 1)
        raw_scores = jnp.einsum(
            "cqhd,ckhd->chqk", query_block, key_rows, preferred_element_type=jnp.float32
        )
        allowed, live_rows = self_masks(first_row, block_rows, clip_len, key_valid)
        logits = jnp.where(allowed, raw_scores * score_scale, MASKED)
        row_max = jnp.max(logits, axis=-1, keepdims=True)
        exponent = jnp.exp(logits - row_max)
        row_sum = jnp.sum(exponent, axis=-1, keepdims=True)
        weights = (exponent / row_sum * live_rows).astype(jnp.bfloat16)
        attended = jnp.einsum(
            "chqk,ckhd->cqhd", weights, value_rows, preferred_element_type=jnp.float32
        )
        return (attended.astype(jnp.bfloat16), row_max + jnp.log(row_sum))

    blocks, log_sums = lax.map(one_block, jnp.arange(length // block_rows, dtype=jnp.int32))
    return (jnp.moveaxis(blocks, 0, 1).reshape(query_rows.shape), log_sums)


def self_backward(query_rows, key_rows, value_rows, grad_rows, log_sums, clip_len, key_valid):
    length = query_rows.shape[1]
    block_rows = min(512, length)
    score_scale = query_rows.shape[3] ** (-0.5)

    def one_block(totals, block_index):
        grad_keys, grad_values = totals
        first_row = block_index * block_rows
        query_block = lax.dynamic_slice_in_dim(query_rows, first_row, block_rows, 1)
        grad_block = lax.dynamic_slice_in_dim(grad_rows, first_row, block_rows, 1)
        raw_scores = jnp.einsum(
            "cqhd,ckhd->chqk", query_block, key_rows, preferred_element_type=jnp.float32
        )
        allowed, live_rows = self_masks(first_row, block_rows, clip_len, key_valid)
        logits = jnp.where(allowed, raw_scores * score_scale, MASKED)
        probs = jnp.exp(logits - log_sums[block_index])
        weights = (probs * live_rows).astype(jnp.bfloat16)
        grad_probs = (
            jnp.einsum(
                "cqhd,ckhd->chqk", grad_block, value_rows, preferred_element_type=jnp.float32
            )
            * live_rows
        )
        row_dot = jnp.sum(probs * grad_probs, axis=-1, keepdims=True)
        grad_scores = (probs * (grad_probs - row_dot)).astype(jnp.bfloat16)
        grad_query = (
            jnp.einsum("chqk,ckhd->cqhd", grad_scores, key_rows, preferred_element_type=jnp.float32)
            * score_scale
        )
        grad_keys = (
            grad_keys
            + jnp.einsum(
                "chqk,cqhd->ckhd", grad_scores, query_block, preferred_element_type=jnp.float32
            )
            * score_scale
        )
        grad_values = grad_values + jnp.einsum(
            "chqk,cqhd->ckhd", weights, grad_block, preferred_element_type=jnp.float32
        )
        return ((grad_keys, grad_values), grad_query)

    zeros = jnp.zeros(key_rows.shape, jnp.float32)
    (grad_keys, grad_values), grad_blocks = lax.scan(
        one_block, (zeros, zeros), jnp.arange(length // block_rows, dtype=jnp.int32)
    )
    grad_query = jnp.moveaxis(grad_blocks, 0, 1).reshape(query_rows.shape)
    return (grad_query, grad_keys, grad_values)


def text_allowed(text_len, text_mask):
    slots = jnp.arange(text_mask.shape[1], dtype=jnp.int32)
    allowed = (slots[None, :] < text_len[:, None]) & ((text_mask > 0) | (slots[None, :] == 0))
    return allowed[:, None, None, :]


def cross_forward(query_rows, key_rows, value_rows, allowed):
    score_scale = query_rows.shape[3] ** (-0.5)
    raw_scores = jnp.einsum(
        "cqhd,ckhd->chqk", query_rows, key_rows, preferred_element_type=jnp.float32
    )
    logits = jnp.where(allowed, raw_scores * score_scale, MASKED)
    row_max = jnp.max(logits, axis=-1, keepdims=True)
    exponent = jnp.exp(logits - row_max)
    row_sum = jnp.sum(exponent, axis=-1, keepdims=True)
    weights = (exponent / row_sum).astype(jnp.bfloat16)
    crossed = jnp.einsum("chqk,ckhd->cqhd", weights, value_rows, preferred_element_type=jnp.float32)
    return (crossed.astype(jnp.bfloat16), row_max + jnp.log(row_sum))


def cross_backward(query_rows, key_rows, value_rows, grad_rows, log_sums, allowed):
    score_scale = query_rows.shape[3] ** (-0.5)
    raw_scores = jnp.einsum(
        "cqhd,ckhd->chqk", query_rows, key_rows, preferred_element_type=jnp.float32
    )
    logits = jnp.where(allowed, raw_scores * score_scale, MASKED)
    probs = jnp.exp(logits - log_sums)
    weights = probs.astype(jnp.bfloat16)
    grad_probs = jnp.einsum(
        "cqhd,ckhd->chqk", grad_rows, value_rows, preferred_element_type=jnp.float32
    )
    row_dot = jnp.sum(probs * grad_probs, axis=-1, keepdims=True)
    grad_scores = (probs * (grad_probs - row_dot)).astype(jnp.bfloat16)
    grad_query = (
        jnp.einsum("chqk,ckhd->cqhd", grad_scores, key_rows, preferred_element_type=jnp.float32)
        * score_scale
    )
    grad_keys = (
        jnp.einsum("chqk,cqhd->ckhd", grad_scores, query_rows, preferred_element_type=jnp.float32)
        * score_scale
    )
    grad_values = jnp.einsum(
        "chqk,cqhd->ckhd", weights, grad_rows, preferred_element_type=jnp.float32
    )
    return (grad_query, grad_keys, grad_values)


def sum_ffn(grad_ffn_in, grad_ffn_out):
    return (
        lax.psum_scatter(grad_ffn_in, ("clip", "frame"), scatter_dimension=0, tiled=True),
        lax.psum_scatter(grad_ffn_out, ("clip", "frame"), scatter_dimension=0, tiled=True),
    )


def sum_attention(
    grad_self_qkv, grad_self_out, grad_cross_qkv, grad_cross_out, grad_gains, grad_shifts
):
    return (
        lax.psum_scatter(grad_self_qkv, ("clip", "frame"), scatter_dimension=0, tiled=True),
        lax.psum_scatter(grad_self_out, ("clip", "frame"), scatter_dimension=0, tiled=True),
        lax.psum_scatter(grad_cross_qkv, ("clip", "frame"), scatter_dimension=0, tiled=True),
        lax.psum_scatter(grad_cross_out, ("clip", "frame"), scatter_dimension=0, tiled=True),
        lax.psum_scatter(grad_gains, ("clip", "frame"), scatter_dimension=1, tiled=True),
        lax.psum_scatter(grad_shifts, ("clip", "frame"), scatter_dimension=1, tiled=True),
    )


def on_device_any(
    hidden_in,
    text_states,
    out_grad,
    self_qkv,
    self_out,
    cross_qkv,
    cross_out,
    ffn_in,
    ffn_out,
    ln_gain,
    ln_bias,
    clip_len,
    frame_mask,
    text_len,
    text_mask,
):
    clip_count, frames, model_width = hidden_in.shape
    text_slots = text_states.shape[1]
    group_count = lax.axis_size("frame")
    columns_here = model_width // group_count
    heads_here = columns_here // HD
    length = frames * group_count
    frame_index = lax.axis_index("frame")
    full_qkv, full_out, full_cross, full_cross_out, gains_low, shifts_low = fetch_attention(
        self_qkv, self_out, cross_qkv, cross_out, ln_gain, ln_bias
    )
    gains = gains_low.astype(jnp.float32)
    shifts = shifts_low.astype(jnp.float32)
    hidden = hidden_in.astype(jnp.float32)
    first_norm, first_pull = jax.vjp(layer_norm, hidden, gains[0], shifts[0])
    first_low = first_norm.astype(jnp.bfloat16)
    query_low = project(first_low, full_qkv[:, 0]).astype(jnp.bfloat16)
    key_low = project(first_low, full_qkv[:, 1]).astype(jnp.bfloat16)
    value_low = project(first_low, full_qkv[:, 2]).astype(jnp.bfloat16)
    query_heads, key_heads, value_heads = (
        lax.all_to_all(query_low, "frame", split_axis=2, concat_axis=1, tiled=True),
        lax.all_to_all(key_low, "frame", split_axis=2, concat_axis=1, tiled=True),
        lax.all_to_all(value_low, "frame", split_axis=2, concat_axis=1, tiled=True),
    )
    head_shape = (clip_count, length, heads_here, HD)
    query_heads = query_heads.reshape(head_shape)
    key_heads = key_heads.reshape(head_shape)
    value_heads = value_heads.reshape(head_shape)
    columns = jnp.arange(length, dtype=jnp.int32)
    key_valid = (columns[None, :] < clip_len[:, None]) & (frame_mask > 0)
    attended_heads, self_sums = self_forward(
        query_heads, key_heads, value_heads, clip_len, key_valid
    )
    attended = lax.all_to_all(
        attended_heads.reshape(clip_count, length, columns_here),
        "frame",
        split_axis=1,
        concat_axis=2,
        tiled=True,
    )
    after_self = hidden + project(attended, full_out)
    second_norm, second_pull = jax.vjp(layer_norm, after_self, gains[1], shifts[1])
    second_low = second_norm.astype(jnp.bfloat16)
    cross_query = project(second_low, full_cross[:, 0]).astype(jnp.bfloat16)
    cross_query_heads = lax.all_to_all(
        cross_query, "frame", split_axis=2, concat_axis=1, tiled=True
    ).reshape(head_shape)
    key_columns = lax.dynamic_slice_in_dim(
        full_cross[:, 1], frame_index * columns_here, columns_here, 1
    )
    value_columns = lax.dynamic_slice_in_dim(
        full_cross[:, 2], frame_index * columns_here, columns_here, 1
    )
    text_shape = (clip_count, text_slots, heads_here, HD)
    text_keys = project(text_states, key_columns).astype(jnp.bfloat16).reshape(text_shape)
    text_values = project(text_states, value_columns).astype(jnp.bfloat16).reshape(text_shape)
    allowed_text = text_allowed(text_len, text_mask)
    crossed_heads, cross_sums = cross_forward(
        cross_query_heads, text_keys, text_values, allowed_text
    )
    crossed = lax.all_to_all(
        crossed_heads.reshape(clip_count, length, columns_here),
        "frame",
        split_axis=1,
        concat_axis=2,
        tiled=True,
    )
    after_cross = after_self + project(crossed, full_cross_out)
    ffn_weight_in, ffn_weight_out = fetch_ffn(ffn_in, ffn_out)
    third_norm, third_pull = jax.vjp(layer_norm, after_cross, gains[2], shifts[2])
    third_low = third_norm.astype(jnp.bfloat16)
    pre_act = project(third_low, ffn_weight_in)
    activated, gelu_pull = jax.vjp(activate, pre_act)
    inner_low = activated.astype(jnp.bfloat16)
    output = (after_cross + project(inner_low, ffn_weight_out)).astype(jnp.bfloat16)
    ffn_weight_in, ffn_weight_out = fetch_ffn(ffn_in, ffn_out)
    grad_ffn_out = weight_grad(inner_low, out_grad)
    (grad_pre,) = gelu_pull(project_back(out_grad, ffn_weight_out))
    grad_pre_low = grad_pre.astype(jnp.bfloat16)
    grad_ffn_in = weight_grad(third_low, grad_pre_low)
    ffn_sums = sum_ffn(grad_ffn_in, grad_ffn_out)
    grad_third, gain_third, shift_third = third_pull(project_back(grad_pre_low, ffn_weight_in))
    grad_after_cross = out_grad.astype(jnp.float32) + grad_third
    full_qkv, full_out, full_cross, full_cross_out, gains_low, shifts_low = fetch_attention(
        self_qkv, self_out, cross_qkv, cross_out, ln_gain, ln_bias
    )
    key_columns = lax.dynamic_slice_in_dim(
        full_cross[:, 1], frame_index * columns_here, columns_here, 1
    )
    value_columns = lax.dynamic_slice_in_dim(
        full_cross[:, 2], frame_index * columns_here, columns_here, 1
    )
    cross_branch = grad_after_cross.astype(jnp.bfloat16)
    grad_cross_out = weight_grad(crossed, cross_branch)
    grad_crossed = project_back(cross_branch, full_cross_out).astype(jnp.bfloat16)
    grad_crossed_heads = lax.all_to_all(
        grad_crossed, "frame", split_axis=2, concat_axis=1, tiled=True
    ).reshape(head_shape)
    grad_cq, grad_tk, grad_tv = cross_backward(
        cross_query_heads, text_keys, text_values, grad_crossed_heads, cross_sums, allowed_text
    )
    grad_tk_low = grad_tk.astype(jnp.bfloat16).reshape(clip_count, text_slots, columns_here)
    grad_tv_low = grad_tv.astype(jnp.bfloat16).reshape(clip_count, text_slots, columns_here)
    text_terms = project_back(grad_tk_low, key_columns) + project_back(grad_tv_low, value_columns)
    grad_text = lax.psum_scatter(
        text_terms.astype(jnp.bfloat16), "frame", scatter_dimension=1, tiled=True
    )
    empty_square = jnp.zeros((model_width, model_width), jnp.float32)
    grad_cross_key = lax.dynamic_update_slice_in_dim(
        empty_square, weight_grad(text_states, grad_tk_low), frame_index * columns_here, 1
    )
    grad_cross_value = lax.dynamic_update_slice_in_dim(
        empty_square, weight_grad(text_states, grad_tv_low), frame_index * columns_here, 1
    )
    grad_cq_low = grad_cq.astype(jnp.bfloat16).reshape(clip_count, length, columns_here)
    grad_cross_query = lax.all_to_all(grad_cq_low, "frame", split_axis=1, concat_axis=2, tiled=True)
    grad_cross_qw = weight_grad(second_low, grad_cross_query)
    grad_second, gain_second, shift_second = second_pull(
        project_back(grad_cross_query, full_cross[:, 0])
    )
    grad_after_self = grad_after_cross + grad_second
    self_branch = grad_after_self.astype(jnp.bfloat16)
    grad_self_out = weight_grad(attended, self_branch)
    grad_attended = project_back(self_branch, full_out).astype(jnp.bfloat16)
    grad_attended_heads = lax.all_to_all(
        grad_attended, "frame", split_axis=2, concat_axis=1, tiled=True
    ).reshape(head_shape)
    grad_query, grad_keys, grad_values = self_backward(
        query_heads, key_heads, value_heads, grad_attended_heads, self_sums, clip_len, key_valid
    )
    flat_shape = (clip_count, length, columns_here)
    grad_query, grad_keys, grad_values = (
        lax.all_to_all(
            grad_query.astype(jnp.bfloat16).reshape(flat_shape),
            "frame",
            split_axis=1,
            concat_axis=2,
            tiled=True,
        ),
        lax.all_to_all(
            grad_keys.astype(jnp.bfloat16).reshape(flat_shape),
            "frame",
            split_axis=1,
            concat_axis=2,
            tiled=True,
        ),
        lax.all_to_all(
            grad_values.astype(jnp.bfloat16).reshape(flat_shape),
            "frame",
            split_axis=1,
            concat_axis=2,
            tiled=True,
        ),
    )
    grad_self_qkv = jnp.stack(
        [
            weight_grad(first_low, grad_query),
            weight_grad(first_low, grad_keys),
            weight_grad(first_low, grad_values),
        ],
        axis=1,
    )
    grad_first_norm = (
        project_back(grad_query, full_qkv[:, 0])
        + project_back(grad_keys, full_qkv[:, 1])
        + project_back(grad_values, full_qkv[:, 2])
    )
    grad_first, gain_first, shift_first = first_pull(grad_first_norm)
    grad_hidden = (grad_after_self + grad_first).astype(jnp.bfloat16)
    grad_cross_qkv = jnp.stack([grad_cross_qw, grad_cross_key, grad_cross_value], axis=1)
    grad_gains = jnp.stack([gain_first, gain_second, gain_third])
    grad_shifts = jnp.stack([shift_first, shift_second, shift_third])
    attn_sums = sum_attention(
        grad_self_qkv, grad_self_out, grad_cross_qkv, grad_cross_out, grad_gains, grad_shifts
    )
    return (
        output,
        grad_hidden,
        grad_text,
        attn_sums[0],
        attn_sums[1],
        attn_sums[2],
        attn_sums[3],
        ffn_sums[0],
        ffn_sums[1],
        attn_sums[4],
        attn_sums[5],
    )


MESH = pl.DeviceIdType.MESH
HBM = pl.BlockSpec(memory_space=pl.ANY)
VMEM = pl.BlockSpec(memory_space=pltpu.VMEM)
SMEM = pl.BlockSpec(memory_space=pltpu.SMEM)
NEG = -1e30
F32 = jnp.float32
BF16 = jnp.bfloat16


def fits(mesh):
    return mesh.shape["clip"] == 4 and mesh.shape["frame"] == 8


class Here:
    def __init__(self):
        self.c = lax.axis_index("clip")
        self.f = lax.axis_index("frame")
        self.core = lax.rem(self.f, 2)
        self.z = lax.div(self.f, 2)
        self.pair = lax.div(self.z, 2)
        self.role = lax.rem(self.z, 2)
        self.group = lax.rem(self.f, 4)
        self.cx = self.c + 1 - 2 * lax.rem(self.c, 2)
        self.cy = lax.rem(self.c + 2, 4)
        self.cd = 3 - self.c
        self.sib = self.f + 1 - 2 * self.core
        self.partner = self.f + 2 - 4 * self.role
        self.far_gate = 2 * (2 - self.pair) + self.core
        self.is_gate = self.role + self.pair == 1
        self.far = [2 * (2 * (1 - self.pair) + j) + self.core for j in range(2)]

    def step(self, d):
        return lax.rem(self.f + d, 8)

    def zstep(self, d):
        return lax.rem(self.f + 2 * d, 8)


class Wire:
    def __init__(self, here, send_sem, recv_sem):
        self.here, self.send_sem, self.recv_sem = here, send_sem, recv_sem
        self.used = 0
        self.open = []

    def copy(self, src, dst, tag, c, f):
        self.used += 1
        return pltpu.make_async_remote_copy(
            src_ref=src,
            dst_ref=dst,
            send_sem=self.send_sem.at[self.used - 1],
            recv_sem=self.recv_sem.at[tag],
            device_id=(c, f),
            device_id_type=MESH,
        )

    def send(self, src, dst, tag, c, f):
        copy = self.copy(src, dst, tag, c, f)
        copy.start()
        self.open.append(copy)

    def arrived(self, dst, tag):
        pltpu.make_async_remote_copy(
            src_ref=dst,
            dst_ref=dst,
            send_sem=self.send_sem.at[0],
            recv_sem=self.recv_sem.at[tag],
            device_id=(self.here.c, self.here.sib),
            device_id_type=MESH,
        ).wait_recv()

    def drain(self):
        for copy in self.open:
            copy.wait_send()
        self.open = []


def call_out(devices):
    barrier = pltpu.get_barrier_semaphore()
    for device in devices:
        pl.semaphore_signal(barrier, inc=1, device_id=device, device_id_type=MESH)


def hear_all(devices):
    pl.semaphore_wait(pltpu.get_barrier_semaphore(), len(devices))


def frame_others(here):
    return [(here.c, here.step(d)) for d in range(1, 8)]


def clip_others(here):
    return [(here.cx, here.f), (here.cy, here.f), (here.cd, here.f)]


class ClipGather:
    def __init__(self, wire, block, tag, own=None):
        self.wire, self.block, self.tag = wire, block, tag
        self.own = own or (lambda half: block(wire.here.c, half))

    def begin(self):
        h, w, b, t, own = self.wire.here, self.wire, self.block, self.tag, self.own
        w.send(own(0), b(h.c, 0), t, h.cx, h.f)
        w.send(own(1), b(h.c, 1), t + 2, h.cy, h.f)
        w.send(own(1), b(h.c, 1), t + 1, h.cx, h.f)
        w.send(own(0), b(h.c, 0), t + 3, h.cy, h.f)

    def middle(self):
        h, w, b, t = self.wire.here, self.wire, self.block, self.tag
        w.arrived(b(h.cx, 0), t)
        w.send(b(h.cx, 0), b(h.cx, 0), t + 4, h.cy, h.f)
        w.arrived(b(h.cy, 1), t + 2)
        w.send(b(h.cy, 1), b(h.cy, 1), t + 5, h.cx, h.f)

    def near(self):
        h, w, b, t = self.wire.here, self.wire, self.block, self.tag
        w.arrived(b(h.cx, 1), t + 1)
        w.arrived(b(h.cy, 0), t + 3)

    def end(self):
        h, w, b, t = self.wire.here, self.wire, self.block, self.tag
        w.arrived(b(h.cd, 0), t + 4)
        w.arrived(b(h.cd, 1), t + 5)


class ZGather:
    def __init__(self, wire, slot, tag, own=None):
        self.wire, self.slot, self.tag = wire, slot, tag
        self.own = own if own is not None else slot(wire.here.f)
        self.open = []

    def step(self, s):
        h, w = self.wire.here, self.wire
        left, right = h.f - 2 * (s - 1), h.f + 2 * (s - 1)
        if s > 1:

            @pl.when(left >= 0)
            def _():
                w.arrived(self.slot(left), self.tag + s - 2)

            @pl.when(right <= 7)
            def _():
                w.arrived(self.slot(right), self.tag + 3 + s - 2)

        if s > 3:
            return
        for block, tag, go, to in (
            (left, self.tag, (left >= 0) & (h.z <= 2), h.f + 2),
            (right, self.tag + 3, (right <= 7) & (h.z >= 1), h.f - 2),
        ):
            src = self.own if s == 1 else self.slot(block)
            copy = w.copy(src, self.slot(block), tag + s - 1, h.c, to)
            pl.when(go)(copy.start)
            self.open.append((go, copy))

    def relay(self, d):
        h, w = self.wire.here, self.wire
        f = h.zstep(d)
        w.send(self.own if d == 0 else self.slot(f), self.slot(f), self.tag + 6 + d, h.c, h.sib)

    def end(self):
        h, w = self.wire.here, self.wire
        for d in range(4):
            w.arrived(self.slot(h.zstep(d) + h.sib - h.f), self.tag + 6 + d)

    def drain(self):
        for go, copy in self.open:
            pl.when(go)(copy.wait_send)


class MatrixGather:
    def __init__(self, wire, block, rows, tag):
        h = wire.here
        self.wire, self.block, self.tag = wire, block, tag
        self.z = ZGather(wire, lambda f: block(h.c, f), tag)
        toward = 2 - 4 * h.pair
        at_end = jnp.logical_not(h.is_gate)
        self.order = [
            h.f,
            h.f + toward,
            jnp.where(at_end, h.f + 2 * toward, h.f - toward),
            jnp.where(at_end, h.f + 3 * toward, h.f + 2 * toward),
        ]
        self.clip = [
            ClipGather(
                wire,
                lambda c, half, f=f: block(c, f).at[pl.ds(rows // 2 * half, rows // 2), :],
                tag + 10 + 6 * d,
            )
            for d, f in enumerate(self.order)
        ]

    def step(self, s):
        self.z.step(s)
        self.clip[s - 1].begin()
        self.z.relay(s - 1) if s == 1 else None
        if s == 4:
            for d in range(1, 4):
                self.z.relay(d)

    def _relay(self, d, i, c):
        h, w = self.wire.here, self.wire
        block = self.block(c, self.order[d])
        w.send(block, block, self.tag + 34 + 3 * d + i, h.c, h.sib)

    def middle(self, d):
        self.clip[d].middle()

    def near(self, d):
        h = self.wire.here
        self.clip[d].near()
        self._relay(d, 0, h.cx)
        self._relay(d, 1, h.cy)

    def last(self, d):
        self.clip[d].end()
        self._relay(d, 2, self.wire.here.cd)

    def end(self):
        h, w = self.wire.here, self.wire
        self.z.end()
        for d in range(4):
            f = self.order[d] + h.sib - h.f
            for i, c in enumerate((h.cx, h.cy, h.cd)):
                w.arrived(self.block(c, f), self.tag + 34 + 3 * d + i)


class ClipScatter:
    def __init__(self, wire, parts, slots, tag):
        self.wire, self.parts, self.slots, self.tag = wire, parts, slots, tag

    def begin(self, which=None):
        h, w, p, s, t = self.wire.here, self.wire, self.parts, self.slots, self.tag
        if which != 1:
            w.send(p(h.cd, 0), s[0], t, h.cx, h.f)
            w.send(p(h.cd, 1), s[1], t + 1, h.cy, h.f)
        if which != 0:
            w.send(p(h.cx, 0), s[2], t + 2, h.cx, h.f)
            w.send(p(h.cy, 1), s[3], t + 3, h.cy, h.f)

    def middle(self):
        h, w, p, s, t = self.wire.here, self.wire, self.parts, self.slots, self.tag
        w.arrived(s[0], t)
        add_into(s[0], p(h.cy, 0))
        w.send(s[0], s[4], t + 4, h.cy, h.f)
        w.arrived(s[1], t + 1)
        add_into(s[1], p(h.cx, 1))
        w.send(s[1], s[5], t + 5, h.cx, h.f)

    def end(self):
        w, s, t = self.wire, self.slots, self.tag
        for i in range(2, 6):
            w.arrived(s[i], t + i)

    def total(self, half):
        s = self.slots
        first, second = (s[2], s[4]) if half == 0 else (s[5], s[3])
        own = self.parts(self.wire.here.c, half)
        return own[...].astype(F32) + first[...].astype(F32) + second[...].astype(F32)


class ZScatter:
    def __init__(self, wire, terms, near, far, tag):
        self.wire, self.terms, self.near, self.far, self.tag = wire, terms, near, far, tag
        self.open = []

    def term(self, m):
        pair = self.wire.here.pair
        return self.terms.at[m + pair * (3 - 2 * m)]

    def _start(self, go, src, dst, tag, f):
        copy = self.wire.copy(src, dst, self.tag + tag, self.wire.here.c, f)
        pl.when(go)(copy.start)
        self.open.append((go, copy))

    def begin(self):
        h = self.wire.here
        for i, m in enumerate((3, 2, 1)):
            self._start(jnp.logical_not(h.is_gate), self.term(m), self.near.at[i], i, h.partner)

    def step(self, s):
        h, w = self.wire.here, self.wire
        block, m, tag, to, f = (
            (self.near.at[0], 3, 0, 0, h.far_gate),
            (self.near.at[1], 2, 1, 1, h.far_gate),
            (self.far.at[0], 0, 3, 0, h.partner),
        )[s - 1]

        @pl.when(h.is_gate)
        def _():
            w.arrived(block, self.tag + tag)
            add_into(block, self.term(m))

        self._start(h.is_gate, block, self.far.at[to], 3 + to, f)

    def end(self):
        h, w = self.wire.here, self.wire

        @pl.when(h.is_gate)
        def _():
            w.arrived(self.near.at[2], self.tag + 2)
            w.arrived(self.far.at[1], self.tag + 4)

        @pl.when(jnp.logical_not(h.is_gate))
        def _():
            w.arrived(self.far.at[0], self.tag + 3)

    def total(self, out):
        h = self.wire.here
        self.end()

        @pl.when(h.is_gate)
        def _():
            others = self.near[2].astype(F32) + self.far[1].astype(F32)
            out[...] = (self.terms[h.z].astype(F32) + others).astype(out.dtype)

        @pl.when(jnp.logical_not(h.is_gate))
        def _():
            out[...] = (self.terms[h.z].astype(F32) + self.far[0].astype(F32)).astype(out.dtype)

    def drain(self):
        for go, copy in self.open:
            pl.when(go)(copy.wait_send)


class SiblingSum:
    def __init__(self, wire, terms, inbox, sums, tag):
        self.wire, self.terms, self.inbox, self.sums, self.tag = wire, terms, inbox, sums, tag

    def begin(self):
        h, w = self.wire.here, self.wire
        for z in range(4):
            w.send(self.terms(2 * z + 1 - h.core), self.inbox(z), self.tag + z, h.c, h.sib)

    def end(self):
        h, w = self.wire.here, self.wire
        for z in range(4):
            w.arrived(self.inbox(z), self.tag + z)
            own, other = self.terms(2 * z + h.core), self.inbox(z)
            self.sums(z)[...] = (own[...].astype(F32) + other[...].astype(F32)).astype(BF16)


def add_into(into, other):
    into[...] = (into[...].astype(F32) + other[...].astype(F32)).astype(BF16)


class LocalCopy:
    def __init__(self, src, through, dst, sem):
        self.a = pltpu.make_async_copy(src, through, sem)
        self.b = pltpu.make_async_copy(through, dst, sem)
        self.a.start()

    def turn(self):
        self.a.wait()
        self.b.start()

    def wait(self):
        self.b.wait()


def comm_call(body, out_shape, in_specs, out_specs, scratch, copies, tags, collective_id, cost=None):
    return pl.pallas_call(
        body,
        out_shape=out_shape,
        in_specs=in_specs,
        out_specs=out_specs,
        scratch_shapes=list(scratch)
        + [pltpu.SemaphoreType.DMA((copies,)), pltpu.SemaphoreType.DMA((tags,))],
        compiler_params=pltpu.CompilerParams(
            collective_id=collective_id, has_side_effects=True, vmem_limit_bytes=60 * 2**20
        ),
    )


def shape(dims, dtype=BF16):
    return jax.ShapeDtypeStruct(dims, dtype)


ROWS = 256


def dot(left, right, contract):
    return lax.dot_general(left, right, ((contract[:1], contract[1:]), ((), ())), preferred_element_type=F32)


def fill_key_bias(bias, clip_len, frame_mask, clip):
    column = lax.broadcasted_iota(jnp.int32, (1, 1024), 1)
    valid = (column < clip_len[clip]) & (frame_mask[pl.ds(clip, 1), :] > 0)
    row = jnp.where(valid, 0.0, NEG).astype(F32)
    bias[...] = jnp.broadcast_to(row, (128, 1024)).T


def text_bias_rows(text_len, text_mask):
    slot = lax.broadcasted_iota(jnp.int32, (1, 128), 1)
    rows = []
    for clip in range(2):
        valid = (slot < text_len[clip]) & ((text_mask[clip : clip + 1, :] > 0) | (slot == 0))
        rows.append(jnp.where(valid, 0.0, NEG).astype(F32))
    return rows


def mask_scores(scores, bias_ref, first, rows):
    low = scores[first:] + bias_ref[first : first + rows, 0:1]
    key = lax.broadcasted_iota(jnp.int32, (rows, rows), 0)
    query = lax.broadcasted_iota(jnp.int32, (rows, rows), 1)
    low = jnp.where(key < query, low, jnp.where(key == query, scores[first:], NEG))
    if first == 0:
        return low
    return jnp.concatenate([scores[:first] + bias_ref[0:first, 0:1], low], axis=0)


def norm_parts(value):
    centered = value - jnp.mean(value, axis=-1, keepdims=True)
    scale = lax.rsqrt(jnp.mean(centered * centered, axis=-1, keepdims=True) + EPSILON)
    return centered * scale, scale


def column_weight(cols, j):
    return cols[:, :, 32 * j : 32 * j + 32, :].reshape(1024, 256)


def attend_rows(i, length, bias, q_ref, k_ref, v_t, o_ref, lse_ref, out_t):
    lane_head = lax.broadcasted_iota(jnp.int32, (ROWS, 256), 1) // HD
    first, n = i * ROWS, (i + 1) * ROWS
    q = q_ref[first:n, :]

    def head(j, _):
        q_head = jnp.where(lane_head == j, q, 0) * jnp.asarray(HD**-0.5, BF16)
        scores = mask_scores(dot(k_ref[0:n, :], q_head, (1, 1)), bias, first, ROWS)
        top = jnp.max(scores, axis=0, keepdims=True)
        weight = jnp.exp(scores - top)
        total = jnp.sum(weight, axis=0, keepdims=True)
        at = pl.ds(pl.multiple_of(j * HD, HD), HD)
        out_t[at, :] = dot(v_t[at, 0:n], weight.astype(BF16), (1, 0)) / total
        lse_ref[pl.ds(j, 1), first:n] = top + jnp.log(total)
        return 0

    lax.fori_loop(0, 4, head, 0)
    live = first + lax.broadcasted_iota(jnp.int32, (ROWS, 256), 0) < length
    o_ref[first:n, :] = jnp.where(live, out_t[...].T, 0).astype(BF16)


def square_of(square, which):
    return square[:, :, 32 * which : 32 * which + 32, :].reshape(1024, 1024)


def text_probs(query, keys, bias, lane_head):
    heads = [jnp.where(lane_head == j, query, 0) for j in range(4)]
    stacked = jnp.concatenate(heads, axis=0)
    scores = dot(stacked, keys, (1, 1)) + bias
    weight = jnp.exp(scores - jnp.max(scores, axis=1, keepdims=True))
    return weight / jnp.sum(weight, axis=1, keepdims=True), stacked


def pick_heads(stacked, lane_head):
    return sum(jnp.where(lane_head == j, stacked[128 * j : 128 * j + 128], 0) for j in range(4))


def forward_body(
    clip_len, text_len, frame_mask, text_mask, gain, shift, self_qkv, cross_qkv, self_out, cross_out,
    text, hid, fin, fout, grad,
    o_hid, o_first, o_q, o_k, o_v, o_heads, o_lse, o_w_a, o_w_b, o_params, o_att, o_tkv, o_square,
    o_second, o_query, o_crossed, o_self, o_cross, o_out, o_in, o_third, o_sum,
    hid_all, first, q_ref, k_ref, v_ref, heads, lse, w_a, w_b, params, att, tkv, sq_self, sq_cross,
    second, query_ref, crossed, after_self, after_cross, out_ref, in_ref,
    out_t, v_t, own_tkv, own_text, own_hid, fin_in, grad_all, win, wout,
    tokens, inner, slope, g_pre, terms, slots, out_w, inbox, sums, near, far,
    bias, cols_a, cols_b, square, placed, local, saved, send_sem, recv_sem,
):
    h = Here()
    w = Wire(h, send_sem, recv_sem)
    partners = frame_others(h) + clip_others(h)
    call_out(partners)
    length = clip_len[h.pair]
    tag = [0]

    def tags(n):
        tag[0] += n
        return tag[0] - n

    T_HID, T_A, T_B, T_FIN, T_AXY, T_BXY = tags(10), tags(7), tags(7), tags(3), tags(6), tags(6)
    T_SELF, T_CROSS, T_ATT, T_TKV, T_WIN, T_GRAD = tags(46), tags(46), tags(8), tags(3), tags(10), tags(6)
    T_TOK, T_WOUT, T_TERM, T_OSIB, T_OZ = tags(6), tags(10), tags(6), tags(4), tags(5)

    def my_columns(f):
        return pl.ds(pl.multiple_of(lax.rem(f, 4) * 256, 256), 256)

    def fin_part(c):
        return fin.at[:, pl.ds(pl.multiple_of(c * 1024, 1024), 1024)]

    spread = lax.broadcasted_iota(jnp.int32, (32, 128), 0) + 32 * lax.rem(h.f, 4)
    spread = jnp.where(spread == lax.broadcasted_iota(jnp.int32, (32, 128), 1), 1.0, 0.0).astype(BF16)
    placed[...] = jnp.zeros_like(placed)
    placed[0:3, :] = dot(gain[...], spread, (1, 0))
    placed[3:6, :] = dot(shift[...], spread, (1, 0))
    for q in range(8):
        group = placed[...] if q % 2 == 0 else jnp.zeros((16, 128), F32)
        cols_a[96:112, 128 * q : 128 * q + 128] = group.astype(BF16)
    for j in range(3):
        cols_a[32 * j : 32 * j + 32, :] = self_qkv[j]
    for j in range(2):
        cols_b[32 * j : 32 * j + 32, :] = cross_qkv[1 + j]
    square[0:32, :] = self_out[...]
    square[32:64, :] = cross_qkv[0]
    square[64:96, :] = cross_out[...]
    own = [
        pltpu.make_async_copy(src, dst, local.at[i])
        for i, (src, dst) in enumerate(
            (
                (cols_a.at[:, my_columns(h.f)], w_a.at[h.c, h.f]),
                (cols_b.at[:, my_columns(h.f)], w_b.at[h.c, h.f]),
                (hid.at[h.pair], hid_all.at[h.f]),
                (square.at[pl.ds(0, 32)], sq_self.at[h.c, h.f]),
                (fin_part(h.c), fin_in.at[h.c]),
                (text, own_text),
                (hid, own_hid),
                (grad, grad_all.at[h.c]),
                (fout, wout.at[h.f]),
                (square.at[pl.ds(32, 64)], sq_cross.at[h.c, h.f]),
            )
        )
    ]
    for copy in own:
        copy.start()
    saves = []

    def save(src, dst):
        copy = pltpu.make_async_copy(src, dst, saved.at[len(saves)])
        copy.start()
        saves.append(copy)

    hear_all(partners)

    own[0].wait()
    for d in (2, 6, 4, 3, 5, 1, 7):
        f = h.step(d)
        w.send(cols_a.at[:, my_columns(f)], w_a.at[h.c, h.f], T_A + d - 1, h.c, f)
    own[7].wait()
    grad_gather = ClipGather(w, lambda c, half: grad_all.at[c, pl.ds(128 * half, 128), :], T_GRAD)
    grad_gather.begin()
    for i, (c, f) in enumerate(clip_others(h)):
        w.send(fin_part(c), fin_in.at[h.c], T_FIN + i, c, f)
    w.send(hid.at[h.pair], hid_all.at[h.f], T_HID, h.c, h.sib)

    def half_of(ref, part):
        return ref.at[pl.ds(64 * part, 64), :]

    for d in range(1, 8):
        w.arrived(w_a.at[h.c, lax.rem(h.f + 8 - d, 8)], T_A + d - 1)
    a_gather = ClipGather(w, lambda c, half: w_a.at[c, pl.ds(4 * half, 4)], T_AXY)
    a_gather.begin()
    for part in range(2):
        w.send(
            half_of(hid.at[1 - h.pair], part),
            half_of(hid_all.at[h.f], part),
            T_HID + 3 + 2 * h.role + part,
            h.c,
            h.far_gate,
        )
        w.send(half_of(hid.at[h.pair], part), half_of(hid_all.at[h.f], part), T_HID + 1 + part, h.c, h.partner)
    own[3].wait()
    self_gather = MatrixGather(w, lambda c, f: sq_self.at[c, f], 32, T_SELF)
    self_gather.step(1)
    forwards = []
    for part in range(2):
        for j in range(2):
            block = half_of(hid_all.at[h.far[j]], part)
            w.arrived(block, T_HID + 3 + 2 * j + part)
            forward = w.copy(block, block, T_HID + 3 + 2 * j + part, h.c, h.partner)
            pl.when(h.is_gate)(forward.start)
            forwards.append(forward)
    self_gather.step(2)
    a_gather.middle()
    for part in range(2):
        w.arrived(half_of(hid_all.at[h.partner], part), T_HID + 1 + part)
    w.send(hid_all.at[h.partner], hid_all.at[h.partner], T_HID + 7, h.c, h.sib)
    for j in range(2):
        w.send(hid_all.at[h.far[j]], hid_all.at[h.far[j]], T_HID + 8 + j, h.c, h.sib)
    self_gather.step(3)
    own[1].wait()
    for d in (2, 6, 4, 3, 5, 1, 7):
        f = h.step(d)
        w.send(cols_b.at[:, my_columns(f)], w_b.at[h.c, h.f], T_B + d - 1, h.c, f)
    fill_key_bias(bias, clip_len, frame_mask, h.pair)
    text_bias = text_bias_rows(text_len, text_mask)
    self_gather.middle(0)
    self_gather.step(4)
    self_gather.middle(1)
    own[9].wait()
    cross_gather = MatrixGather(w, lambda c, f: sq_cross.at[c, f], 64, T_CROSS)
    a_gather.near()
    a_gather.end()
    grad_gather.middle()
    cross_gather.step(1)
    own[4].wait()
    for i, (c, f) in enumerate(clip_others(h)):
        w.arrived(fin_in.at[c], T_FIN + i)
    win_gather = ZGather(w, lambda f: win.at[:, f], T_WIN, fin_in)
    win_copy = pltpu.make_async_copy(fin_in, win.at[:, h.f], local.at[11])
    win_copy.start()
    win_gather.step(1)
    win_gather.relay(0)
    for g in range(8):
        group = sum(w_a[g // 2, 4 * (g % 2) + i, 96:104, 0:128].astype(F32) for i in range(4))
        params[:, 128 * g : 128 * g + 128] = group
    own[2].wait()
    w.arrived(hid_all.at[h.sib], T_HID)
    w.arrived(hid_all.at[h.partner + h.sib - h.f], T_HID + 7)
    for j in range(2):
        w.arrived(hid_all.at[h.far[j] + h.sib - h.f], T_HID + 8 + j)

    def project_rows(i, _):
        at = pl.ds(pl.multiple_of(i * 256, 256), 256)
        rows = hid_all[pl.ds(2 * i, 2)].reshape(256, 1024).astype(F32)
        xhat, _ = norm_parts(rows)
        low = (xhat * params[0:1, :] + params[3:4, :]).astype(BF16)
        first[at, :] = low
        for j, out in enumerate((q_ref, k_ref, v_ref)):
            out[at, :] = dot(low, column_weight(w_a, j), (1, 0)).astype(BF16)
        return 0

    lax.fori_loop(0, 2, project_rows, 0)
    self_gather.middle(2)
    for d in range(1, 8):
        w.arrived(w_b.at[h.c, lax.rem(h.f + 8 - d, 8)], T_B + d - 1)
    b_gather = ClipGather(w, lambda c, half: w_b.at[c, pl.ds(4 * half, 4)], T_BXY)
    b_gather.begin()
    cross_gather.step(2)
    lax.fori_loop(2, 4, project_rows, 0)
    v_t[...] = v_ref[...].T
    win_gather.step(2)
    self_gather.middle(3)
    cross_gather.step(3)
    b_gather.middle()

    def att_slot(f):
        return att.at[lax.div(f, 4), :, my_columns(f)]

    att_sends = []

    def attend_and_send(i):
        attend_rows(i, length, bias, q_ref, k_ref, v_t, heads, lse, out_t)
        for f in (2 * i, 2 * i + 1):
            block = heads.at[pl.ds(128 * f, 128), :]
            away = h.f != f
            copy = w.copy(block, att_slot(h.f), T_ATT + h.f, h.c, f)
            stay = pltpu.make_async_copy(block, att_slot(h.f), local.at[12])
            pl.when(away)(copy.start)
            pl.when(jnp.logical_not(away))(stay.start)
            att_sends.append((away, copy, stay))

    attend_and_send(3)
    def text_slot(f):
        return tkv.at[:, :, :, my_columns(f)]

    b_gather.near()
    b_gather.end()
    own[5].wait()
    for clip in range(2):
        for j in range(2):
            own_tkv[clip, j] = dot(own_text[clip], column_weight(w_b, j), (1, 0)).astype(BF16)
    w.send(own_tkv, text_slot(h.f), T_TKV, h.c, h.partner)
    w.send(own_tkv, text_slot(h.f), T_TKV + 1, h.c, h.sib)
    text_copy = pltpu.make_async_copy(own_tkv, text_slot(h.f), local.at[10])
    text_copy.start()
    cross_gather.step(4)
    win_gather.step(3)
    cross_gather.middle(0)
    attend_and_send(2)
    for d in range(4):
        self_gather.near(d)
        self_gather.last(d)
    cross_gather.middle(1)
    w.arrived(text_slot(h.partner), T_TKV)
    w.send(text_slot(h.partner), text_slot(h.partner), T_TKV + 2, h.c, h.sib)
    attend_and_send(1)
    win_gather.step(4)
    for d in range(1, 4):
        win_gather.relay(d)
    cross_gather.middle(2)
    attend_and_send(0)
    cross_gather.middle(3)
    for src, dst in (
        (hid_all, o_hid), (first, o_first), (q_ref, o_q), (k_ref, o_k), (v_ref, o_v), (heads, o_heads), (lse, o_lse),
        (w_a, o_w_a), (w_b, o_w_b), (params, o_params),
    ):
        save(src, dst)
    self_gather.end()
    for d in range(1, 8):
        f = lax.rem(h.f + 8 - d, 8)
        w.arrived(att_slot(f), T_ATT + f)
    for away, _, stay in att_sends:
        pl.when(jnp.logical_not(away))(stay.wait)

    own[6].wait()
    value = own_hid[...].reshape(256, 1024).astype(F32) + dot(
        att[...].reshape(256, 1024), square_of(sq_self, 0), (1, 0)
    )
    after_self[...] = value
    xhat, _ = norm_parts(value)
    second[...] = (xhat * params[1:2, :] + params[4:5, :]).astype(BF16)
    for d in range(4):
        cross_gather.near(d)
        cross_gather.last(d)
    cross_gather.end()
    query_ref[...] = dot(second[...], square_of(sq_cross, 0), (1, 0)).astype(BF16)
    w.arrived(text_slot(h.sib), T_TKV + 1)
    w.arrived(text_slot(h.partner + h.sib - h.f), T_TKV + 2)
    text_copy.wait()
    lane_head = lax.broadcasted_iota(jnp.int32, (128, 256), 1) // HD
    for clip in range(2):
        for group in range(4):
            rows, columns = pl.ds(128 * clip, 128), pl.ds(256 * group, 256)
            query = query_ref[rows, columns] * jnp.asarray(HD**-0.5, BF16)
            probs, _ = text_probs(query, tkv[clip, 0, :, columns], text_bias[clip], lane_head)
            part = dot(probs.astype(BF16), tkv[clip, 1, :, columns], (1, 0))
            crossed[rows, columns] = pick_heads(part, lane_head).astype(BF16)
    own[8].wait()
    out_gather = ZGather(w, lambda f: wout.at[f], T_WOUT)
    out_gather.step(1)
    out_gather.relay(0)
    value = after_self[...] + dot(crossed[...], square_of(sq_cross, 1), (1, 0))
    after_cross[...] = value
    xhat, _ = norm_parts(value)
    tokens[h.c] = (xhat * params[2:3, :] + params[5:6, :]).astype(BF16)

    token_gather = ClipGather(w, lambda c, half: tokens.at[c, pl.ds(128 * half, 128), :], T_TOK)
    token_gather.begin()
    for src, dst in (
        (att, o_att), (tkv, o_tkv), (second, o_second), (query_ref, o_query), (crossed, o_crossed),
        (after_self, o_self), (after_cross, o_cross),
    ):
        save(src, dst)
    save(sq_self, o_square.at[0])
    for which in range(2):
        save(sq_cross.at[:, :, pl.ds(32 * which, 32), :], o_square.at[1 + which])
    win_copy.wait()
    win_gather.end()

    def hidden(c):
        def part(i, _):
            rows = pl.ds(pl.multiple_of(128 * i, 128), 128)
            pre = dot(tokens[c, rows, :], win[...].reshape(1024, 1024), (1, 0))
            cdf = 0.5 * (1.0 + lax.erf(pre * (0.5**0.5)))
            inner[c, rows, :] = (pre * cdf).astype(BF16)
            slope[c, rows, :] = cdf + pre * jnp.exp(-0.5 * pre * pre) * 0.3989422804014327
            return 0

        lax.fori_loop(0, 2, part, 0)

    def hidden_back(c):
        g_inner = dot(grad_all[c], wout[...].reshape(1024, 1024), (1, 1))
        g_pre[c] = (g_inner * slope[c]).astype(BF16)
        terms[c] = dot(g_pre[c], win[...].reshape(1024, 1024), (1, 1)).astype(BF16)

    def out_terms(c):
        out_ref[c] = dot(inner[c], wout[...].reshape(1024, 1024), (1, 0)).astype(BF16)

    sibling = SiblingSum(w, lambda f: out_w.at[f], lambda z: inbox.at[z], lambda z: sums.at[z], T_OSIB)
    z_scatter = ZScatter(w, sums, near, far, T_OZ)
    tall = (1024, 1024)

    def out_weight(i, _):
        columns = pl.ds(pl.multiple_of(i * 256, 256), 256)
        out = dot(inner[:, :, columns].reshape(1024, 256), grad_all[...].reshape(tall), (0, 0))
        out_w[pl.ds(2 * i, 2)] = out.astype(BF16).reshape(2, 128, 1024)
        return 0

    def in_weight(i, _):
        columns = pl.ds(pl.multiple_of(i * 256, 256), 256)
        out = dot(tokens[:, :, columns].reshape(1024, 256), g_pre[...].reshape(tall), (0, 0))
        in_ref[:, pl.ds(pl.multiple_of(32 * i, 32), 32), :] = out.astype(BF16).reshape(8, 32, 1024)
        return 0

    hidden(h.c)
    out_gather.step(2)
    grad_gather.near()
    grad_gather.end()
    token_gather.middle()
    token_gather.near()
    out_gather.step(3)

    def both(i, _):
        hidden(jnp.where(i == 0, h.cx, h.cy))
        return 0

    lax.fori_loop(0, 2, both, 0)
    out_gather.step(4)
    for d in range(1, 4):
        out_gather.relay(d)
    token_gather.end()
    hidden(h.cd)
    lax.fori_loop(0, 4, out_weight, 0)
    sibling.begin()
    out_gather.end()
    scatter = ClipScatter(
        w, lambda c, half: terms.at[c, pl.ds(128 * half, 128), :], [slots.at[i] for i in range(6)], T_TERM
    )
    hidden_back(h.cd)
    scatter.begin(0)
    sibling.end()
    z_scatter.begin()

    def others_back(i, _):
        hidden_back(jnp.where(i == 0, h.cx, h.cy))
        return 0

    lax.fori_loop(0, 2, others_back, 0)
    scatter.begin(1)
    hidden_back(h.c)
    scatter.middle()
    z_scatter.step(1)
    lax.fori_loop(0, 2, in_weight, 0)
    lax.fori_loop(2, 4, in_weight, 0)
    save(in_ref, o_in)
    z_scatter.step(2)
    z_scatter.step(3)

    def out_term(i, _):
        out_terms(i)
        return 0

    lax.fori_loop(0, 4, out_term, 0)
    save(out_ref, o_out)
    scatter.end()
    for half in range(2):
        o_third[128 * half : 128 * half + 128, :] = scatter.total(half)
    z_scatter.total(o_sum)
    w.drain()
    for copy in forwards:
        pl.when(h.is_gate)(copy.wait_send)
    for away, copy, _ in att_sends:
        pl.when(away)(copy.wait_send)
    for one in (self_gather.z, cross_gather.z, win_gather, out_gather, z_scatter):
        one.drain()
    for copy in saves:
        copy.wait()


def forward(*args):
    column, rows, full, quarter = (1024, 256), (256, 1024), (4, 256, 1024), (4, 128, 1024)
    kept = [
        shape((8, 128, 1024)),
        shape((1024, 1024)),
        shape(column),
        shape(column),
        shape(column),
        shape(column),
        shape((8, 1024), F32),
        shape((4, 8, 112, 256)),
        shape((4, 8, 64, 256)),
        shape((8, 1024), F32),
        shape((2, 128, 1024)),
        shape((2, 2, 128, 1024)),
        shape((4, 8, 96, 1024)),
        shape(rows),
        shape(rows),
        shape(rows),
        shape(rows, F32),
        shape(rows, F32),
        shape(full),
        shape((8, 128, 1024)),
    ]
    scratch = [pltpu.VMEM(one.shape, one.dtype) for one in kept]
    scratch[12:13] = [pltpu.VMEM((4, 8, rows, 1024), BF16) for rows in (32, 64)]
    kept[12] = shape((3, 4, 8, 32, 1024))
    return comm_call(
        forward_body,
        tuple(kept) + (shape(rows, F32), shape((128, 1024), F32)),
        [SMEM] * 2 + [VMEM] * 8 + [HBM] * 5,
        (HBM,) * len(kept) + (VMEM,) * 2,
        scratch
        + [
            pltpu.VMEM((256, ROWS), F32),
            pltpu.VMEM((256, 1024), BF16),
            pltpu.VMEM((2, 2, 128, 256), BF16),
            pltpu.VMEM((2, 128, 1024), BF16),
            pltpu.VMEM((2, 128, 1024), BF16),
            pltpu.VMEM((4, 32, 1024), BF16),
            pltpu.VMEM(full, BF16),
            pltpu.VMEM((4, 8, 32, 1024), BF16),
            pltpu.VMEM((8, 128, 1024), BF16),
            pltpu.VMEM(full, BF16),
            pltpu.VMEM(full, BF16),
            pltpu.VMEM(full, F32),
            pltpu.VMEM(full, BF16),
            pltpu.VMEM(full, BF16),
            pltpu.VMEM((6, 128, 1024), BF16),
            pltpu.VMEM((8, 128, 1024), BF16),
            pltpu.VMEM(quarter, BF16),
            pltpu.VMEM(quarter, BF16),
            pltpu.VMEM((3, 128, 1024), BF16),
            pltpu.VMEM((2, 128, 1024), BF16),
            pltpu.VMEM((1024, 128), F32),
            pltpu.VMEM((112, 1024), BF16),
            pltpu.VMEM((64, 1024), BF16),
            pltpu.VMEM((96, 1024), BF16),
            pltpu.VMEM((16, 128), F32),
            pltpu.SemaphoreType.DMA((13,)),
            pltpu.SemaphoreType.DMA((24,)),
        ],
        216,
        192,
        1,
    )(*args)


def attend_back_rows(i, length, bias, q_ref, k_ref, v_ref, o_ref, lse_ref, g_ref, dq_ref, dq_t, k_t, dk, dv):
    lane_head = lax.broadcasted_iota(jnp.int32, (ROWS, 256), 1) // HD
    first, n = i * ROWS, (i + 1) * ROWS
    q = q_ref[first:n, :] * jnp.asarray(HD**-0.5, BF16)
    live = first + lax.broadcasted_iota(jnp.int32, (ROWS, 256), 0) < length
    g = jnp.where(live, g_ref[first:n, :], 0)
    both = (g.astype(F32) * o_ref[first:n, :].astype(F32)).T
    row_dots = jnp.concatenate(
        [jnp.sum(both[HD * j : HD * j + HD], axis=0, keepdims=True) for j in range(4)], axis=0
    )
    lse = lse_ref[0:4, first:n]

    def pick(rows, j):
        at = lax.broadcasted_iota(jnp.int32, rows.shape, 0) == j
        return jnp.sum(jnp.where(at, rows, 0), axis=0, keepdims=True)

    def head(j, _):
        q_head = jnp.where(lane_head == j, q, 0)
        g_head = jnp.where(lane_head == j, g, 0)
        scores = mask_scores(dot(k_ref[0:n, :], q_head, (1, 1)), bias, first, ROWS)
        probs = jnp.exp(scores - pick(lse, j))
        grads = dot(v_ref[0:n, :], g_head, (1, 1))
        dlogits = (probs * (grads - pick(row_dots, j))).astype(BF16)
        dv[0:n, :] += dot(probs.astype(BF16), g_head, (1, 0))
        dk[0:n, :] += dot(dlogits, q_head, (1, 0))
        at = pl.ds(pl.multiple_of(j * HD, HD), HD)
        dq_t[at, :] = dot(k_t[at, 0:n], dlogits, (1, 0))
        return 0

    lax.fori_loop(0, 4, head, 0)
    dq_ref[first:n, :] = (dq_t[...].T * (HD**-0.5)).astype(BF16)


def norm_back(xhat, scale, grad, gain):
    h = grad * gain
    return scale * (
        h
        - jnp.mean(h, axis=-1, keepdims=True)
        - xhat * jnp.mean(h * xhat, axis=-1, keepdims=True)
    )


def backward_body(
    clip_len, text_len, frame_mask, text_mask, norms_in,
    h_third, h_out, h_cross, h_self, h_second, h_query, h_crossed, h_att, h_square, h_tkv, h_out_terms, h_in_terms,
    h_q, h_k, h_v, h_o, h_lse, h_hid, h_first, h_wa, h_wb, h_text, h_own,
    o_output, o_in, o_hidden, o_square, o_qkv, o_ckv, o_norm, o_text,
    v_third, v_out, after_cross, query_ref, crossed, att, mats, tkv, out_terms,
    q_ref, k_ref, v_ref, o_ref, lse, w_a, w_b, text_in,
    g_crossed, g_att, g_after, slots, t_inbox, t_near, t_far, t_total,
    i_inbox, i_near, i_far, i_out, i_in,
    g_square, s_inbox, s_slots, s_part, y_part, z_near, z_far, y_near, y_far,
    g_heads, dq_t, k_t, dk, dv, d_cols, f_inbox, f_in,
    a_terms, a_slots, a_sum, a_in, b_terms, b_slots, b_sum, b_in,
    t_terms, tt_in, n_row, n_terms, n_slots, n_sum, n_in,
    bias, loaded, local, send_sem, recv_sem,
):
    h = Here()
    w = Wire(h, send_sem, recv_sem)
    partners = frame_others(h) + clip_others(h)
    call_out(partners)
    length = clip_len[h.pair]
    tag = [0]

    def tags(n):
        tag[0] += n
        return tag[0] - n

    loads = []

    def load(src, dst):
        copy = pltpu.make_async_copy(src, dst, loaded.at[len(loads)])
        copy.start()
        loads.append(copy)
        return copy

    l_terms = load(h_out_terms, out_terms)
    own_terms = [mats.at[0, z, pl.ds(0, 4)] for z in range(4)]
    l_own = [load(h_in_terms.at[2 * z + h.core], own_terms[z]) for z in range(4)]
    l_third, l_cross = load(h_third, v_third), load(h_cross, after_cross)
    l_out, l_m2 = load(h_out, v_out), load(h_square.at[2], mats.at[2])
    l_middle = [load(*pair) for pair in ((h_crossed, crossed), (h_query, query_ref), (h_tkv, tkv))]
    l_m1 = load(h_square.at[1], mats.at[1])
    l_att = load(h_att, att)
    l_heads = [
        load(*pair)
        for pair in (
            (h_q, q_ref), (h_k, k_ref), (h_v, v_ref), (h_o, o_ref), (h_lse, lse), (h_wb, w_b), (h_text, text_in),
            (h_wa, w_a),
        )
    ]
    fill_key_bias(bias, clip_len, frame_mask, h.pair)
    text_bias = text_bias_rows(text_len, text_mask)
    hear_all(partners)

    def matrix(which):
        return mats[which].reshape(1024, 1024)

    out_scatter = ClipScatter(
        w,
        lambda c, half: out_terms.at[c, pl.ds(128 * half, 128), :],
        [slots.at[i] for i in range(6)],
        tags(6),
    )
    in_tag = tags(4)
    for z in range(4):
        w.send(h_in_terms.at[2 * z + 1 - h.core], i_inbox.at[z], in_tag + z, h.c, h.sib)
    in_scatter = ZScatter(w, i_inbox, i_near, i_far, tags(5))
    l_terms.wait()
    out_scatter.begin()

    def square_sums(which):
        sibling = SiblingSum(
            w,
            lambda f: g_square.at[which, :, f],
            lambda z: s_inbox.at[which, z],
            lambda z: s_inbox.at[which, z],
            tags(4),
        )
        clip = ClipScatter(
            w,
            lambda c, half: s_inbox.at[which, :, c, pl.ds(16 * half, 16), :],
            [s_slots.at[which, i] for i in range(6)],
            tags(6),
        )
        return sibling, clip

    squares = [square_sums(which) for which in range(3)]

    def put(which, value):
        g_square[which] = value.astype(BF16).reshape(4, 8, 32, 1024)

    def columns_of(f):
        return pl.ds(pl.multiple_of(lax.rem(f, 4) * 256, 256), 256)

    def part_of(f):
        return g_att.at[lax.div(f, 4), :, columns_of(f)]

    def text_part(f):
        return g_text.at[lax.div(f, 4), :, :, columns_of(f)]

    for copy in (l_third, l_cross, l_out):
        copy.wait()
    xhat, scale = norm_parts(after_cross[...])
    grad = v_third[...]
    gain_third = jnp.sum(grad * xhat, axis=0, keepdims=True)
    shift_third = jnp.sum(grad, axis=0, keepdims=True)
    n_row[...] = jnp.zeros_like(n_row)
    n_row[2:3, :] = gain_third
    n_row[5:6, :] = shift_third
    g_after_cross = v_out[...].reshape(256, 1024).astype(F32) + norm_back(xhat, scale, grad, norms_in[2:3, :])
    g_after[...] = g_after_cross
    after_self, own_hid = v_third, v_out
    l_self, l_own_hid = load(h_self, after_self), load(h_own, own_hid)
    branch = g_after_cross.astype(BF16)
    l_m2.wait()
    g_crossed[...] = dot(branch, matrix(2), (1, 1)).astype(BF16)
    l_first = load(h_first, mats.at[2])
    for copy in l_middle + l_own:
        copy.wait()
    put(2, dot(crossed[...], branch, (0, 0)))
    squares[2][0].begin()
    second = crossed
    l_second = load(h_second, second)
    for z in range(4):
        w.arrived(i_inbox.at[z], in_tag + z)
        add_into(i_inbox.at[z], own_terms[z])
    in_scatter.begin()
    l_m0 = load(h_square.at[0], mats.at[0])
    g_query, g_text = query_ref, tkv
    lane_head = lax.broadcasted_iota(jnp.int32, (128, 256), 1) // HD
    for clip in range(2):
        for group in range(4):
            rows, columns = pl.ds(128 * clip, 128), pl.ds(256 * group, 256)
            keys, values = tkv[clip, 0, :, columns], tkv[clip, 1, :, columns]
            query = query_ref[rows, columns] * jnp.asarray(HD**-0.5, BF16)
            probs, stacked = text_probs(query, keys, text_bias[clip], lane_head)
            grads = g_crossed[rows, columns]
            g_stacked = jnp.concatenate([jnp.where(lane_head == j, grads, 0) for j in range(4)], axis=0)
            g_probs = dot(g_stacked, values, (1, 1))
            row_dot = jnp.sum(probs * g_probs, axis=1, keepdims=True)
            g_logits = (probs * (g_probs - row_dot)).astype(BF16)
            part = dot(g_logits, keys, (1, 0))
            g_query[rows, columns] = (pick_heads(part, lane_head) * (HD**-0.5)).astype(BF16)
            g_text[clip, 0, :, columns] = dot(g_logits, stacked, (0, 0)).astype(BF16)
            g_text[clip, 1, :, columns] = dot(probs.astype(BF16), g_stacked, (0, 0)).astype(BF16)
        if clip == 0:
            out_scatter.middle()
            in_scatter.step(1)
            squares[2][0].end()
            squares[2][1].begin()
    text_sibling = SiblingSum(w, text_part, lambda z: t_inbox.at[z], lambda z: t_inbox.at[z], tags(4))
    text_sibling.begin()
    l_m1.wait()
    grad = dot(g_query[...], matrix(1), (1, 1))
    l_hid = load(h_hid, mats.at[1])
    l_self.wait()
    xhat, scale = norm_parts(after_self[...])
    n_row[1:2, :] = jnp.sum(grad * xhat, axis=0, keepdims=True)
    n_row[4:5, :] = jnp.sum(grad, axis=0, keepdims=True)
    g_after_self = g_after[...] + norm_back(xhat, scale, grad, norms_in[1:2, :])
    g_after[...] = g_after_self
    branch = g_after_self.astype(BF16)
    l_m0.wait()
    g_att[...] = dot(branch, matrix(0), (1, 1)).astype(BF16).reshape(2, 128, 1024)
    heads_tag = tags(7)
    for d in (4, 2, 6, 3, 5, 1, 7):
        f = h.step(d)
        w.send(part_of(f), g_heads.at[h.f], heads_tag + d - 1, h.c, f)
    own_part = pltpu.make_async_copy(part_of(h.f), g_heads.at[h.f], local.at[0])
    own_part.start()
    in_scatter.step(2)
    in_scatter.step(3)
    l_second.wait()
    l_att.wait()
    put(1, dot(second[...], g_query[...], (0, 0)))
    squares[1][0].begin()
    put(0, dot(att[...].reshape(256, 1024), branch, (0, 0)))
    squares[0][0].begin()
    text_sibling.end()
    text_scatter = ZScatter(w, t_inbox, t_near, t_far, tags(5))
    text_scatter.begin()
    squares[2][1].middle()
    squares[1][0].end()
    squares[1][1].begin()
    out_scatter.end()
    for half in range(2):
        rows = pl.ds(128 * half, 128)
        o_output[rows, :] = (after_cross[rows, :] + out_scatter.total(half)).astype(BF16)
    squares[0][0].end()
    squares[0][1].begin()
    in_scatter.total(i_out)
    i_tag = tags(3)
    for i, (c, f) in enumerate(clip_others(h)):
        w.send(i_out.at[c], i_in.at[h.c], i_tag + i, c, f)
    i_in[h.c] = i_out[h.c]
    squares[1][1].middle()

    def square_part(which, out, row):
        squares[which][1].end()
        for half in range(2):
            total = squares[which][1].total(half)
            out[:, row + 16 * half : row + 16 * half + 16, :] = total.astype(BF16)

    text_scatter.step(1)
    for copy in l_heads:
        copy.wait()
    k_t[...] = k_ref[...].T
    dk[...] = jnp.zeros_like(dk)
    dv[...] = jnp.zeros_like(dv)
    for d in range(1, 8):
        w.arrived(g_heads.at[lax.rem(h.f + 8 - d, 8)], heads_tag + d - 1)
    own_part.wait()
    g_rows = g_heads[...].reshape(1024, 256)

    def rows_back(i):
        attend_back_rows(
            i, length, bias, q_ref, k_ref, v_ref, o_ref, lse, g_rows, d_cols.at[0], dq_t, k_t, dk, dv
        )

    text_scatter.step(2)
    text_scatter.step(3)
    squares[0][1].middle()
    rows_back(0)
    square_part(2, s_part, 32)
    square_part(1, s_part, 0)
    z_scatter = ZScatter(w, s_part, z_near, z_far, tags(5))
    z_scatter.begin()
    rows_back(1)

    class Columns:
        def __init__(self, terms, slots, sums, inbox):
            self.sums, self.inbox, self.tag = sums, inbox, tags(13)
            self.clip = ClipScatter(
                w,
                lambda c, half: terms.at[c, pl.ds(4 * half, 4)],
                [slots.at[i] for i in range(6)],
                self.tag,
            )

        def spread(self):
            self.clip.end()
            for half in range(2):
                self.sums[4 * half : 4 * half + 4] = self.clip.total(half).astype(BF16)
            for d in (4, 2, 6, 3, 5, 1, 7):
                f = h.step(d)
                w.send(self.sums.at[f], self.inbox.at[h.f], self.tag + 5 + d, h.c, f)
            self.inbox[h.f] = self.sums[h.f]

        def wait(self):
            for d in range(1, 8):
                w.arrived(self.inbox.at[lax.rem(h.f + 8 - d, 8)], self.tag + 5 + d)

    text_scatter.total(t_total)
    g_tkv = [t_total[j].astype(BF16) for j in range(2)]
    text = text_in[h.pair]
    for j in range(2):
        b_terms[:, :, 32 * j : 32 * j + 32, :] = (
            dot(text, g_tkv[j], (0, 0)).astype(BF16).reshape(4, 8, 32, 256)
        )
    b_columns = Columns(b_terms, b_slots, b_sum, b_in)
    b_columns.clip.begin()
    t_terms[...] = (
        dot(g_tkv[0], column_weight(w_b, 0), (1, 1)) + dot(g_tkv[1], column_weight(w_b, 1), (1, 1))
    ).astype(BF16)
    tt_tag = tags(7)
    for d in range(1, 8):
        f = h.step(d)
        w.send(
            t_terms.at[pl.ds(pl.multiple_of(f * 16, 16), 16), :], tt_in.at[h.f], tt_tag + d - 1, h.c, f
        )
    tt_in[h.f] = t_terms[pl.ds(pl.multiple_of(h.f * 16, 16), 16), :]
    z_scatter.step(1)
    rows_back(2)
    square_part(0, y_part, 0)
    y_scatter = ZScatter(w, y_part, y_near, y_far, tags(5))
    y_scatter.begin()
    z_scatter.step(2)
    z_scatter.step(3)
    b_columns.clip.middle()
    rows_back(3)
    d_cols[1] = dk[...].astype(BF16)
    d_cols[2] = dv[...].astype(BF16)
    l_first.wait()
    a_columns = [Columns(a_terms.at[j], a_slots.at[j], a_sum.at[j], a_in.at[j]) for j in range(3)]
    for j in range(3):
        a_terms[j] = dot(mats[2].reshape(1024, 1024), d_cols[j], (0, 0)).astype(BF16).reshape(4, 8, 32, 256)
        a_columns[j].clip.begin()
    y_scatter.step(1)

    f_terms = mats.at[0]
    f_sibling = SiblingSum(
        w,
        lambda f: f_terms.at[lax.div(f, 2), pl.ds(pl.multiple_of(lax.rem(f, 2) * 4, 4), 4)],
        lambda z: f_inbox.at[z],
        lambda z: f_inbox.at[z],
        tags(4),
    )
    l_hid.wait()

    def frame_terms(i, _):
        rows = pl.ds(pl.multiple_of(i * 256, 256), 256)
        grad = sum(dot(d_cols[j, rows, :], column_weight(w_a, j), (1, 1)) for j in range(3))
        f_terms[i] = grad.astype(BF16).reshape(8, 32, 1024)
        xhat, _ = norm_parts(mats[1, i].reshape(256, 1024).astype(F32))
        n_row[0:1, :] += jnp.sum(grad * xhat, axis=0, keepdims=True)
        n_row[3:4, :] += jnp.sum(grad, axis=0, keepdims=True)
        return 0

    lax.fori_loop(0, 4, frame_terms, 0)
    f_sibling.begin()
    y_scatter.step(2)
    a_columns[0].clip.middle()
    f_sibling.end()
    f_tag = tags(4)
    other = 2 * (1 - h.pair)
    is_end = jnp.logical_not(h.is_gate)
    to_gate, to_far = [], []
    for j in range(2):
        to_gate.append(w.copy(f_inbox.at[other + j], f_in.at[1 + j], f_tag + 1 + j, h.c, h.partner))
        pl.when(is_end)(to_gate[j].start)
    w.send(f_inbox.at[lax.div(h.partner, 2)], f_in.at[0], f_tag, h.c, h.partner)
    for c in range(4):
        for f in range(8):
            group = 2 * c + f // 4
            n_terms[c, f] = n_row[:, 128 * group : 128 * group + 128].astype(BF16)
    n_columns = Columns(n_terms, n_slots, n_sum, n_in)
    n_columns.clip.begin()
    a_columns[1].clip.middle()
    a_columns[0].spread()
    for j in range(2):

        @pl.when(h.is_gate)
        def _():
            w.arrived(f_in.at[1 + j], f_tag + 1 + j)
            add_into(f_inbox.at[other + j], f_in.at[1 + j])

        to_far.append(w.copy(f_inbox.at[other + j], f_in.at[3], f_tag + 3, h.c, h.far[j]))
        pl.when(h.is_gate)(to_far[j].start)
    a_columns[2].clip.middle()
    a_columns[1].spread()
    n_columns.clip.middle()
    y_scatter.step(3)
    a_columns[2].spread()
    n_columns.spread()
    b_columns.spread()
    z_scatter.total(o_square.at[pl.ds(32, 64), :])
    for i, (c, f) in enumerate(clip_others(h)):
        w.arrived(i_in.at[c], i_tag + i)
    for c in range(4):
        o_in[:, 1024 * c : 1024 * c + 1024] = i_in[c].astype(F32)
    for d in range(1, 8):
        w.arrived(tt_in.at[lax.rem(h.f + 8 - d, 8)], tt_tag + d - 1)
    for p in range(2):
        o_text[p] = sum(tt_in[4 * p + q].astype(F32) for q in range(4)).astype(BF16)
    y_scatter.total(o_square.at[pl.ds(0, 32), :])
    w.arrived(f_in.at[0], f_tag)
    w.arrived(f_in.at[3], f_tag + 3)

    def hidden_out(clip, total):
        xhat, scale = norm_parts(own_hid[clip].astype(F32))
        rows = pl.ds(pl.multiple_of(clip * 128, 128), 128)
        o_hidden[clip] = (g_after[rows, :] + norm_back(xhat, scale, total, norms_in[0:1, :])).astype(BF16)

    l_own_hid.wait()
    hidden_out(h.pair, (f_inbox[h.z].astype(F32) + f_in[0].astype(F32)).reshape(128, 1024))
    hidden_out(1 - h.pair, f_in[3].astype(F32).reshape(128, 1024))
    for j in range(3):
        a_columns[j].wait()
        for q in range(4):
            o_qkv[j, :, 256 * q : 256 * q + 256] = a_in[j, q].astype(F32) + a_in[j, 4 + q].astype(F32)
    b_columns.wait()
    for j in range(2):
        for q in range(4):
            at = pl.ds(32 * j, 32)
            o_ckv[j, :, 256 * q : 256 * q + 256] = b_in[q, at, :].astype(F32) + b_in[4 + q, at, :].astype(F32)
    n_columns.wait()
    o_norm[...] = sum(n_in[f].astype(F32) for f in range(8))
    w.drain()
    for one in (in_scatter, text_scatter, z_scatter, y_scatter):
        one.drain()
    for j in range(2):
        pl.when(is_end)(to_gate[j].wait_send)
        pl.when(h.is_gate)(to_far[j].wait_send)


def backward(*args):
    def buffer(*dims):
        return pltpu.VMEM(dims, BF16)

    def full(*dims):
        return pltpu.VMEM(dims, F32)

    return comm_call(
        backward_body,
        (
            shape((256, 1024)),
            shape((32, 4096), F32),
            shape((2, 128, 1024)),
            shape((96, 1024), F32),
            shape((3, 32, 1024), F32),
            shape((2, 32, 1024), F32),
            shape((16, 128), F32),
            shape((2, 16, 1024)),
        ),
        [SMEM] * 2 + [VMEM] * 3 + [HBM] * 23,
        (VMEM,) * 8,
        [
            full(256, 1024), buffer(2, 128, 1024), full(256, 1024), buffer(256, 1024), buffer(256, 1024),
            buffer(2, 128, 1024), buffer(3, 4, 8, 32, 1024), buffer(2, 2, 128, 1024), buffer(4, 256, 1024),
            buffer(1024, 256), buffer(1024, 256), buffer(1024, 256), buffer(1024, 256), full(8, 1024),
            buffer(4, 8, 112, 256), buffer(4, 8, 64, 256), buffer(2, 128, 1024),
            buffer(256, 1024), buffer(2, 128, 1024), full(256, 1024),
            buffer(6, 128, 1024), buffer(4, 2, 128, 256), buffer(3, 2, 128, 256), buffer(2, 2, 128, 256),
            full(2, 128, 256),
            buffer(4, 4, 32, 1024), buffer(3, 4, 32, 1024), buffer(2, 4, 32, 1024),
            buffer(4, 32, 1024), buffer(4, 32, 1024),
            buffer(3, 4, 8, 32, 1024), buffer(3, 4, 4, 32, 1024), buffer(3, 6, 4, 16, 1024),
            buffer(4, 64, 1024), buffer(4, 32, 1024), buffer(3, 64, 1024), buffer(2, 64, 1024),
            buffer(3, 32, 1024), buffer(2, 32, 1024),
            buffer(8, 128, 256), full(256, ROWS), buffer(256, 1024), full(1024, 256), full(1024, 256),
            buffer(3, 1024, 256), buffer(4, 4, 32, 1024), buffer(4, 4, 32, 1024),
            buffer(3, 4, 8, 32, 256), buffer(3, 6, 4, 32, 256), buffer(3, 8, 32, 256), buffer(3, 8, 32, 256),
            buffer(4, 8, 64, 256), buffer(6, 4, 64, 256), buffer(8, 64, 256), buffer(8, 64, 256),
            buffer(128, 1024), buffer(8, 16, 1024), full(16, 1024), buffer(4, 8, 16, 128), buffer(6, 4, 16, 128),
            buffer(8, 16, 128), buffer(8, 16, 128), full(1024, 128),
            pltpu.SemaphoreType.DMA((32,)),
            pltpu.SemaphoreType.DMA((1,)),
        ],
        208,
        160,
        2,
    )(*args)


def finish_body(*refs):
    ins, outs = refs[:9], refs[9:]
    output, hidden, text, qkv, square, ckv, fin, fout, norm = ins
    o_output, o_hidden, o_text, o_qkv, o_self_out, o_cross, o_cross_out, o_fin, o_fout, o_gain, o_shift = outs
    o_fout[...] = fout[...]
    o_output[...] = output[...].reshape(2, 128, 1024)
    o_hidden[...] = hidden[...]
    o_text[...] = text[...]
    o_fin[...] = fin[...]
    o_qkv[...] = qkv[...]
    o_self_out[...] = square[0:32, :]
    o_cross[0] = square[32:64, :]
    o_cross[1:3] = ckv[...]
    o_cross_out[...] = square[64:96, :]
    place = lax.rem(lax.axis_index("frame"), 4)
    for row, out in ((0, o_gain), (3, o_shift)):
        out[...] = sum(
            jnp.where(place == i, norm[row : row + 3, 32 * i : 32 * i + 32], 0) for i in range(4)
        )


def finish(*args):
    return pl.pallas_call(
        finish_body,
        out_shape=(
            shape((2, 128, 1024)),
            shape((2, 128, 1024)),
            shape((2, 16, 1024)),
            shape((3, 32, 1024), F32),
            shape((32, 1024), F32),
            shape((3, 32, 1024), F32),
            shape((32, 1024), F32),
            shape((32, 4096), F32),
            shape((128, 1024), F32),
            shape((3, 32), F32),
            shape((3, 32), F32),
        ),
        in_specs=[VMEM] * 9,
        out_specs=(VMEM,) * 11,
        compiler_params=pltpu.CompilerParams(vmem_limit_bytes=60 * 2**20),
    )(*args)


def on_device_fast(
    hidden_in,
    text_states,
    out_grad,
    self_qkv,
    self_out,
    cross_qkv,
    cross_out,
    ffn_in,
    ffn_out,
    ln_gain,
    ln_bias,
    clip_len,
    frame_mask,
    text_len,
    text_mask,
):
    (
        hid_all, first_low, query, key, value, att_heads, lse, w_a, w_b, params, att, tkv, square,
        second, cross_query, crossed, after_self, after_cross, out_terms, in_terms, third_sum, grad_ffn_out,
    ) = forward(
        clip_len, text_len, frame_mask, text_mask, ln_gain, ln_bias, jnp.moveaxis(self_qkv, 1, 0),
        jnp.moveaxis(cross_qkv, 1, 0), self_out, cross_out, text_states, hidden_in, ffn_in, ffn_out, out_grad.reshape(256, 1024),
    )
    output, grad_ffn_in, grad_hidden, square_sum, qkv_sum, ckv_sum, norm_sum, grad_text = backward(
        clip_len, text_len, frame_mask, text_mask, params,
        third_sum, out_grad, after_cross, after_self, second, cross_query, crossed, att, square, tkv,
        out_terms, in_terms.reshape(8, 4, 32, 1024), query, key, value, att_heads, lse,
        hid_all.reshape(4, 8, 32, 1024), first_low.reshape(4, 8, 32, 1024), w_a, w_b, text_states, hidden_in,
    )
    results = finish(output, grad_hidden, grad_text, qkv_sum, square_sum, ckv_sum, grad_ffn_in, grad_ffn_out, norm_sum)
    output, grad_hidden, grad_text, qkv, g_self_out, cross, g_cross_out, grad_ffn_in, grad_ffn_out, gains, shifts = results
    return (
        output,
        grad_hidden,
        grad_text,
        jnp.moveaxis(qkv, 0, 1),
        g_self_out,
        jnp.moveaxis(cross, 0, 1),
        g_cross_out,
        grad_ffn_in,
        grad_ffn_out,
        gains,
        shifts,
    )


def solution(mesh):
    return jax.shard_map(
        on_device_fast if fits(mesh) else on_device_any,
        mesh=mesh,
        in_specs=(
            P("clip", "frame", None),
            P("clip", None, None),
            P("clip", "frame", None),
            P(("clip", "frame"), None, None),
            P(("clip", "frame"), None),
            P(("clip", "frame"), None, None),
            P(("clip", "frame"), None),
            P(("clip", "frame"), None),
            P(("clip", "frame"), None),
            P(None, ("clip", "frame")),
            P(None, ("clip", "frame")),
            P("clip"),
            P("clip", None),
            P("clip"),
            P("clip", None),
        ),
        out_specs=(
            P("clip", "frame", None),
            P("clip", "frame", None),
            P("clip", "frame", None),
            P(("clip", "frame"), None, None),
            P(("clip", "frame"), None),
            P(("clip", "frame"), None, None),
            P(("clip", "frame"), None),
            P(("clip", "frame"), None),
            P(("clip", "frame"), None),
            P(None, ("clip", "frame")),
            P(None, ("clip", "frame")),
        ),
        check_vma=False,
    )
```

profile of v0, /device:TPU:0, one launch (start us, length us, event | category | flops | bytes accessed | tf_op | source)
XLA Modules:
  0.0 267.3 jit_solution(12227250811365981945)
XLA Ops:
  0.6 156.8 %shard_map.230 = (bf16[8,128,1024]{2,1,0:T(8,128)(2,1)}, bf16[1024,1024]{1,0:T(8,128)(2,1)}, bf16[1024,256]{1,0:T(8,128)(2,1)}, bf16[1024,256]{1,0:T(8,128)(2,1)...) custom-call(s32[2]{0:T(128)} %clip_len.3, ...), custom_call_target="tpu_custom_call" | custom-call | tf_op jit(solution)/shard_map/pallas_call | solution.py:1282
  157.5 106.0 %shard_map.231 = (bf16[256,1024]{1,0:T(8,128)(2,1)}, f32[32,4096]{1,0:T(8,128)}, bf16[2,128,1024]{2,1,0:T(8,128)(2,1)}, f32[96,1024]{1,0:T(8,128)}, f32[3,32,102...) custom-call(s32[2]{0:T(128)} %clip_len.3, s32[2]{0:T(128)} %text_len.3, ...), custom_call_target="tpu_custom_call" | custom-call | tf_op jit(solution)/shard_map/pallas_call | solution.py:1756
  263.5 3.6 %shard_map.232 = (bf16[2,128,1024]{2,1,0:T(8,128)(2,1)}, bf16[2,128,1024]{2,1,0:T(8,128)(2,1)}, bf16[2,16,1024]{2,1,0:T(8,128)(2,1)}, f32[3,32,1024]{2,1,0:T(8,1...) custom-call(bf16[256,1024]{1,0:T(8,128)(2,1)} %get-tuple-element.73., ...), custom_call_target="tpu_custom_call" | custom-call | tf_op jit(solution)/shard_map/pallas_call | solution.py:1820
where the time goes:
time: 271 us; the launch traced here: 267 us
  Pallas kernels  266 us (98%)
    pallas_call x1, Pallas kernels, forward(): comm_call(forward_body, tuple(kept) + (shape(rows, F32), shape((128, 1024...  157 us
    pallas_call x1, Pallas kernels, backward(): comm_call(backward_body, (shape((256, 1024)), shape((32, 4096), F32), sha...  106 us

commit v1 on v0

--- a/solution.py
+++ b/solution.py
@@ -1641,6 +1641,7 @@
     z_scatter.step(3)
     b_columns.clip.middle()
     rows_back(3)
+    b_columns.spread()
     d_cols[1] = dk[...].astype(BF16)
     d_cols[2] = dv[...].astype(BF16)
     l_first.wait()
@@ -1705,7 +1706,6 @@
     y_scatter.step(3)
     a_columns[2].spread()
     n_columns.spread()
-    b_columns.spread()
     z_scatter.total(o_square.at[pl.ds(32, 64), :])
     for i, (c, f) in enumerate(clip_others(h)):
         w.arrived(i_in.at[c], i_tag + i)

time: 271 us -> 268 us (0.989)
  Pallas kernels: 266 us -> 263 us
    pallas_call x1, Pallas kernels: 106 us -> 103 us  [backward(): comm_call(backward_body, (shape((256, 1024)), shape((32, 4096), F32), sha...]
where the time goes in v1:
time: 268 us; the launch traced here: 264 us
  Pallas kernels  263 us (98%)
    pallas_call x1, Pallas kernels, forward(): comm_call(forward_body, tuple(kept) + (shape(rows, F32), shape((128, 1024...  157 us
    pallas_call x1, Pallas kernels, backward(): comm_call(backward_body, (shape((256, 1024)), shape((32, 4096), F32), sha...  103 us

profile of v1, /device:TPU:0, one launch (start us, length us, event | category | flops | bytes accessed | tf_op | source)
XLA Modules:
  0.0 264.1 jit_solution(170421855839475082)
XLA Ops:
  0.6 156.8 %shard_map.230 = (bf16[8,128,1024]{2,1,0:T(8,128)(2,1)}, bf16[1024,1024]{1,0:T(8,128)(2,1)}, bf16[1024,256]{1,0:T(8,128)(2,1)}, bf16[1024,256]{1,0:T(8,128)(2,1)...) custom-call(s32[2]{0:T(128)} %clip_len.3, ...), custom_call_target="tpu_custom_call" | custom-call | tf_op jit(solution)/shard_map/pallas_call | solution.py:1282
  157.5 102.9 %shard_map.231 = (bf16[256,1024]{1,0:T(8,128)(2,1)}, f32[32,4096]{1,0:T(8,128)}, bf16[2,128,1024]{2,1,0:T(8,128)(2,1)}, f32[96,1024]{1,0:T(8,128)}, f32[3,32,102...) custom-call(s32[2]{0:T(128)} %clip_len.3, s32[2]{0:T(128)} %text_len.3, ...), custom_call_target="tpu_custom_call" | custom-call | tf_op jit(solution)/shard_map/pallas_call | solution.py:1756
  260.4 3.6 %shard_map.232 = (bf16[2,128,1024]{2,1,0:T(8,128)(2,1)}, bf16[2,128,1024]{2,1,0:T(8,128)(2,1)}, bf16[2,16,1024]{2,1,0:T(8,128)(2,1)}, f32[3,32,1024]{2,1,0:T(8,1...) custom-call(bf16[256,1024]{1,0:T(8,128)(2,1)} %get-tuple-element.73., ...), custom_call_target="tpu_custom_call" | custom-call | tf_op jit(solution)/shard_map/pallas_call | solution.py:1820
